TPU v7x, 512 devices: a whole 4x8x8 slice. The times are simulated.
512 devices in a mesh: dp: 32 (over y, x), gene: 16 (over z, core).
Axes of the slice: x: 4, y: 8, z: 8, core: 2. Of those that a mesh axis runs over, the one named last changes fastest.
Arguments:
- labels: int32 [32768], P('dp'), may hold values from 0 to 511, as said below
- counts: int32 [32768, 16384], P('dp', 'gene'), may hold values from 0 to 39
- library_size: int32 [32768], P('dp'), may hold values from 2000 to 29999
- loadings: bfloat16 [16384, 256], P('gene'), may hold values from -0.046875 to 0.046875
Outputs:
- normalized: bfloat16 [512, 16384], P(('dp', 'gene'))
- scores: float32 [512, 256], P(('dp', 'gene'))
Inputs may be any that keep to these rules, and one draw needn't show every extreme that they name: Within each device's block of 1024 cells the labels do not fall; every group has at least one cell.
All inputs are finite; a program needn't handle non-finite values.
Results may differ from a plain program's by a relative error of at most 0.0065.
Values may be sent and summed in bfloat16 or wider, within the bound.
No kernel may reach another device: no remote copies, remote signals or barrier semaphores. Data moves between devices by JAX's collectives and lax.ppermute only.
A program may use at most 64 MiB of HBM per device.

v0:
```python
import jax
import jax.numpy as jnp
from jax import lax
from jax.sharding import PartitionSpec as P

G = 512


def dense_sums(labels, counts_bf, groups):
    members = lax.broadcasted_iota(jnp.int32, (groups, labels.shape[0]), 0) == labels[None, :]
    return jnp.dot(members.astype(jnp.bfloat16), counts_bf, preferred_element_type=jnp.float32)


def shards(labels, counts, library_size, loadings):
    groups = G
    counts_bf = counts.astype(jnp.bfloat16)
    partial_value = dense_sums(labels, counts_bf, groups)
    members = lax.broadcasted_iota(jnp.int32, (groups, labels.shape[0]), 0) == labels[None, :]
    library_part = jnp.sum(
        jnp.where(members, library_size.astype(jnp.float32)[None, :], 0.0), axis=1
    )
    pseudo, library = (
        lax.psum_scatter(partial_value, "dp", scatter_dimension=0, tiled=True),
        lax.psum_scatter(library_part, "dp", scatter_dimension=0, tiled=True),
    )
    normalized = jnp.log(1.0 + 10000.0 * pseudo / library[:, None]).astype(jnp.bfloat16)
    partial_scores = jnp.dot(normalized, loadings, preferred_element_type=jnp.float32)
    scores = lax.psum_scatter(partial_scores, "gene", scatter_dimension=0, tiled=True)
    group_major = lax.all_to_all(normalized, "gene", split_axis=0, concat_axis=1, tiled=True)
    return (group_major, scores)


def solution(mesh):
    placed = (P("dp"), P("dp", "gene"), P("dp"), P("gene", None))
    return jax.shard_map(
        shards,
        mesh=mesh,
        in_specs=placed,
        out_specs=(P(("dp", "gene"), None), P(("dp", "gene"), None)),
        check_vma=False,
    )
```

profile of v0, /device:TPU:1, one launch (start us, length us, event | category | flops | bytes accessed | tf_op | source)
XLA Modules:
  0.0 311.6 jit_solution(15286502716927065972)
XLA Ops:
  7.2 0.0 copy-start
  7.2 0.0 reduce-scatter.2.cloned.1.call-start
  7.2 4.9 %fusion = f32[512,1024]{1,0:T(8,128)} fusion(s32[1024,1024]{1,0:T(8,128)} %param.5, s32[1024]{0:T(1024)} %param.4), kind=kOutput, calls=%fused_computation.1 | convolution fusion | flops 1075314688 | bytes 6295552 | tf_op jit(solution)/shard_map/dot_general | solution.py:11
  12.1 0.0 copy-start.1
  12.1 0.0 reduce-scatter.2.cloned.1.call-update
  12.1 0.7 copy-done.1
  12.8 1.3 dynamic-slice
  14.0 1.3 dynamic-slice.2
  16.0 0.0 copy-done.2
  16.0 0.3 select_reduce_fusion
  16.3 62.0 %all-reduce = f32[512]{0:T(512)S(1)} all-reduce(f32[512]{0:T(512)S(1)} %select_reduce_fusion), channel_id=3, replica_groups=mesh['dp'=32,'gene'=16] {'dp'}, use_global_device_ids=true, to_apply=%region_2.3.clone | all-reduce | flops 512 | bytes 4096
  78.3 0.1 dynamic-slice.1
  78.4 155.7 %reduce-scatter.2.cloned.1.call-done = f32[16,1024]{1,0:T(8,128)} async-done(((f32[512,1024]{1,0:T(8,128)}), f32[16,1024]{1,0:T(8,128)}) %reduce-scatter.2.cloned.1.call-update) | async-done | bytes 65552 | tf_op jit(solution)/shard_map/reduce_scatter | solution.py:23
  234.1 0.0 copy-done
  234.1 1.1 fusion.3
  235.2 48.8 %all-reduce.1 = f32[16,256]{1,0:T(8,128)S(1)} all-reduce(f32[16,256]{1,0:T(8,128)S(1)} %fusion.3), channel_id=4, replica_groups=mesh['dp'=32,'gene'=16] {'gene'}, use_global_device_ids=true, to_apply=%region_3.4.clone | all-reduce | flops 4096 | bytes 32768
  284.0 0.9 fusion.6
  285.0 0.5 broadcast.3
  285.5 0.7 reduce
  286.1 0.6 reshape.15
  286.8 10.0 %all-to-all-start = ((bf16[16,2,512]{2,1,0:T(2,128)(2,1)}), bf16[16,2,512]{2,1,0:T(2,128)(2,1)S(1)}, u32[]{:S(2)}, u32[]{:S(2)}) async-start(bf16[16,2,512]{2,1,0:T(2,128)(2,1)} %reshape.15), calls=%async_computation.1 | async-start | bytes 65536 | tf_op jit(solution)/shard_map/all_to_all | solution.py:29
  296.7 1.2 constant_dynamic-slice_fusion
  297.9 6.2 %all-to-all-done = bf16[16,2,512]{2,1,0:T(2,128)(2,1)S(1)} async-done(((bf16[16,2,512]{2,1,0:T(2,128)(2,1)}), bf16[16,2,512]{2,1,0:T(2,128)(2,1)S(1)}, u32[]{:S(2)}, u32[]{:S(2)}) %all-to-all-start) | async-done | bytes 32800 | tf_op jit(solution)/shard_map/all_to_all | solution.py:29
  304.1 0.7 reshape.16
  (2 shorter events, 0.0 us)
Async XLA Ops:
  7.2 227.0 %copy-start = (bf16[1024,256]{1,0:T(8,128)(2,1)S(1)}, bf16[1024,256]{1,0:T(8,128)(2,1)}, u32[]{:S(2)}) copy-start(bf16[1024,256]{1,0:T(8,128)(2,1)} %param.7) | copy-start | bytes 1572868
  7.2 226.9 %reduce-scatter.2.cloned.1.call-start = ((), (), s32[]{:S(2)}) async-start(), calls=%async_computation.2 | async-start | bytes 2162688 | tf_op jit(solution)/shard_map/reduce_scatter | solution.py:23
  12.1 0.7 copy-start.1
  12.1 3.9 %copy-start.2 = (s32[1024]{0:T(1024)S(1)}, s32[1024]{0:T(1024)}, u32[]{:S(2)}) copy-start(s32[1024]{0:T(1024)} %param.4) | copy-start | bytes 12292
  286.8 17.4 %all-to-all-start = ((bf16[16,2,512]{2,1,0:T(2,128)(2,1)}), bf16[16,2,512]{2,1,0:T(2,128)(2,1)S(1)}, u32[]{:S(2)}, u32[]{:S(2)}) async-start(bf16[16,2,512]{2,1,0:T(2,128)(2,1)} %reshape.15), calls=%async_computation.1 | async-start | bytes 65536 | tf_op jit(solution)/shard_map/all_to_all | solution.py:29
Sparse Core Ops, SparseCore 0:
  12.4 221.6 reduce-scatter.1
where the time goes:
time: 312 us
  waiting for transfers between devices  162 us (52%)
  blocking collectives  111 us (36%)
  between operations  14.7 us (5%)
  starting transfers between devices  10 us (3%)
  local copies, waits for them, and re-layouts  6.31 us (2%)
  matrix products  5.93 us (2%)
    reduce_scatter x1, waiting for transfers between devices, shards(): lax.psum_scatter(partial_value, 'dp', scatter_dimension=0, tiled=True)  156 us
    unnamed x2, blocking collectives  111 us
    all_to_all x1, starting transfers between devices, shards(): lax.all_to_all(normalized, 'gene', split_axis=0, concat_axis=1, tiled=True)  9.97 us
  transfers between devices with their start and end apart: 2, of which 2 were waited for; matrix products, arithmetic and copies ran while one was open for 1% of the time, Pallas kernels for 0%

commit v1 on v0

v1 whole, which is shorter than its diff:
```python
import jax
import jax.numpy as jnp
from jax import lax
from jax.sharding import PartitionSpec as P

G = 512
F32 = jnp.float32
BF16 = jnp.bfloat16


def split3(value):
    one = value.astype(BF16)
    rest = value - one.astype(F32)
    two = rest.astype(BF16)
    return one, two, (rest - two.astype(F32)).astype(BF16)


def shards(labels, counts, library_size, loadings):
    cells = labels.shape[0]
    genes = counts.shape[1]
    k = loadings.shape[1]
    members = lax.broadcasted_iota(jnp.int32, (G, cells), 0) == labels[None, :]
    partial_value = jnp.dot(members.astype(BF16), counts.astype(BF16), preferred_element_type=F32)
    library_part = jnp.sum(jnp.where(members, library_size.astype(F32)[None, :], 0.0), axis=1)
    lib = jnp.stack(split3(library_part), axis=1)
    sent = jnp.concatenate([partial_value.astype(BF16), jnp.pad(lib, ((0, 0), (0, 125)))], axis=1)
    got = lax.all_to_all(sent, "dp", 0, 0, tiled=True)
    summed = jnp.sum(got.reshape(32, 16, genes + 128).astype(F32), axis=0)
    pseudo = summed[:, :genes]
    library = jnp.sum(summed[:, genes:], axis=1)
    normalized = jnp.log(1.0 + 10000.0 * pseudo / library[:, None]).astype(BF16)
    partial_scores = jnp.dot(normalized, loadings, preferred_element_type=F32)
    sent = jnp.concatenate([normalized, *split3(partial_scores)], axis=1)
    got = lax.all_to_all(sent.reshape(16, -1, 128), "gene", 0, 0, tiled=True)
    rows = genes // 128
    group_major = got[:, :rows].reshape(1, 16 * genes)
    scores = jnp.sum(got[:, rows:].astype(F32).reshape(16, 3, k), axis=(0, 1))[None]
    return (group_major, scores)


def solution(mesh):
    placed = (P("dp"), P("dp", "gene"), P("dp"), P("gene", None))
    return jax.shard_map(
        shards,
        mesh=mesh,
        in_specs=placed,
        out_specs=(P(("dp", "gene"), None), P(("dp", "gene"), None)),
        check_vma=False,
    )
```

time: 312 us -> 70.5 us (0.23)
  waiting for transfers between devices: 162 us -> 0 us
  blocking collectives: 111 us -> 62.1 us
  between operations: 14.7 us -> 0.72 us
  starting transfers between devices: 10 us -> 0 us
  local copies, waits for them, and re-layouts: 6.31 us -> 0.91 us
    reduce_scatter x1 -> x0, waiting for transfers between devices: 156 us -> none  [shards(): lax.psum_scatter(partial_value, 'dp', scatter_dimension=0, tiled=True)]
    unnamed x2 -> x0, blocking collectives: 111 us -> none
    all_to_all x0 -> x2, blocking collectives: none -> 62.1 us  [the longest x1 41.3 us: shards(): got = lax.all_to_all(sent, 'dp', 0, 0, tiled=True)]
    all_to_all x1 -> x0, starting transfers between devices: 9.97 us -> none  [shards(): lax.all_to_all(normalized, 'gene', split_axis=0, concat_axis=1, tiled=True)]
    all_to_all x1 -> x0, waiting for transfers between devices: 6.2 us -> none  [shards(): lax.all_to_all(normalized, 'gene', split_axis=0, concat_axis=1, tiled=True)]
    unnamed x12 -> x2, local copies, waits for them, and re-layouts: 5.8 us -> 0.01 us
  transfers between devices with their start and end apart: 2 -> 0, of which waited for: 2 -> 0; matrix products, arithmetic and copies ran while one was open for 1% -> 0% of each run, Pallas kernels for 0% -> 0%
where the time goes in v1:
time: 70.5 us; the launch traced here: 70.3 us
  blocking collectives  62.1 us (88%)
  matrix products  3.65 us (5%)
  other arithmetic  2.83 us (4%)
  local copies, waits for them, and re-layouts  0.91 us (1%)
  between operations  0.72 us (1%)
    all_to_all x1, blocking collectives, shards(): got = lax.all_to_all(sent, 'dp', 0, 0, tiled=True)  41.3 us
    all_to_all x1, blocking collectives, shards(): got = lax.all_to_all(sent.reshape(16, -1, 128), 'gene', 0, 0, tiled=True)  20.8 us
    dot_general x1, matrix products, shards(): jnp.dot(members.astype(BF16), counts.astype(BF16), preferred_element_type...  3.47 us

profile of v1, /device:TPU:1, one launch (start us, length us, event | category | flops | bytes accessed | tf_op | source)
XLA Modules:
  0.0 70.3 jit_solution(1274412702350197974)
XLA Ops:
  0.6 0.0 copy-start
  0.6 0.7 %convert_element_type.104 = f32[1024]{0:T(1024)S(1)} convert(s32[1024]{0:T(1024)} %param.6) | non-fusion elementwise | flops 1024 | bytes 8192 | tf_op jit(solution)/shard_map/convert_element_type | solution.py:24
  1.4 1.0 %select_reduce_fusion = f32[512]{0:T(512)S(1)} fusion(f32[1024]{0:T(1024)S(1)} %convert_element_type.104, s32[1024]{0:T(1024)} %param.4), kind=kLoop, calls=%fused_computation.3 | loop fusion | flops 1572352 | bytes 10240 | tf_op jit(solution)/shard_map/reduce_sum | solution.py:24
  2.4 0.2 copy.9
  2.6 3.5 %fusion.3 = bf16[512,1024]{1,0:T(8,128)(2,1)S(1)} fusion(s32[1024,1024]{1,0:T(8,128)} %param.5, s32[1024]{0:T(1024)} %param.4), kind=kOutput, calls=%fused_computation.7 | convolution fusion | flops 1075838976 | bytes 5246976 | tf_op jit(solution)/shard_map/dot_general | solution.py:23
  6.1 0.1 fusion.6
  6.2 41.3 %all_to_all.14 = bf16[32,16,1152]{2,1,0:T(8,128)(2,1)S(1)} all-to-all(bf16[32,16,1152]{2,1,0:T(8,128)(2,1)S(1)} %bitcast.5), channel_id=1, replica_groups=mesh['dp'=32,'gene'=16] {'dp'}, dimensions={0} | all-to-all | bytes 2359296 | tf_op jit(solution)/shard_map/all_to_all | solution.py:27
  47.5 0.2 convert_reduce_fusion
  47.7 0.1 slice_reduce_fusion
  47.8 0.1 fusion.11
  47.9 0.0 copy-done
  47.9 0.2 fusion.14
  48.1 0.1 reshape.52
  48.2 20.8 %all_to_all.15 = bf16[16,14,128]{2,1,0:T(8,128)(2,1)S(1)} all-to-all(bf16[16,14,128]{2,1,0:T(8,128)(2,1)S(1)} %reshape.52), channel_id=1, replica_groups=mesh['dp'=32,'gene'=16] {'gene'}, dimensions={0} | all-to-all | bytes 114688 | tf_op jit(solution)/shard_map/all_to_all | solution.py:34
  69.0 0.6 reshape.53
  69.7 0.6 reduce_sum.51
  (7 shorter events, 0.1 us)
Async XLA Ops:
  0.6 47.3 %copy-start = (bf16[1024,256]{1,0:T(8,128)(2,1)S(1)}, bf16[1024,256]{1,0:T(8,128)(2,1)}, u32[]{:S(2)}) copy-start(bf16[1024,256]{1,0:T(8,128)(2,1)} %param.7) | copy-start | bytes 1572868

commit v2 on v1

v2 whole, which is shorter than its diff:
```python
import jax
import jax.numpy as jnp
from jax import lax
from jax.experimental import pallas as pl
from jax.experimental.pallas import tpu as pltpu
from jax.sharding import PartitionSpec as P

G = 512
F32 = jnp.float32
BF16 = jnp.bfloat16
LANES = 128
OWN = 16
FIRST = [[(2 * h + l) * 4 + x for l in range(2) for x in range(4)] for h in range(4)]
SECOND = [[(2 * h + l) * 4 + x for h in range(4)] for l in range(2) for x in range(4)]
VMEM = pl.BlockSpec(memory_space=pltpu.VMEM)
LIMIT = 48 * 1024 * 1024


def split3(value):
    one = value.astype(BF16).astype(F32)
    two = (value - one).astype(BF16).astype(F32)
    return one, two, ((value - one) - two).astype(BF16).astype(F32)


def in_lanes(pieces, lane):
    return jnp.where(lane == 0, pieces[0], jnp.where(lane == 1, pieces[1], jnp.where(lane == 2, pieces[2], 0.0)))


def sums_kernel(labels_ref, lib_ref, counts_ref, out_ref, members_ref):
    step = pl.program_id(0)
    cells = counts_ref.shape[0]
    width = counts_ref.shape[1]
    tiles = width // LANES

    @pl.when(step == 0)
    def _():
        group = lax.broadcasted_iota(jnp.int32, (G, cells), 0)
        members_ref[...] = (group == labels_ref[...].reshape(1, cells)).astype(F32).astype(BF16)
        size = lib_ref[...].reshape(1, cells)
        high = size // 256
        low = size - high * 256
        part = jnp.where(lax.broadcasted_iota(jnp.int32, (2 * LANES, cells), 0) < LANES, high, low)
        both = lax.dot_general(
            members_ref[...], part.astype(F32).astype(BF16), (((1,), (1,)), ((), ())), preferred_element_type=F32
        )
        total = both[:, :LANES] * 256.0 + both[:, LANES:]
        lane = lax.broadcasted_iota(jnp.int32, (G, LANES), 1)
        placed = in_lanes(split3(total), lane % 4)
        lane = lax.broadcasted_iota(jnp.int32, (OWN, LANES), 1) // 4
        for m in range(8):
            tile = jnp.zeros((OWN, LANES), F32)
            for h in range(4):
                at = (h * 8 + m) * OWN
                tile = jnp.where(lane == h, placed[at : at + OWN], tile)
            out_ref[m, out_ref.shape[1] - OWN :, :] = tile.astype(BF16)

    sums = jnp.dot(members_ref[...], counts_ref[...].astype(F32).astype(BF16), preferred_element_type=F32)
    sums = sums.astype(BF16)
    for m in range(8):
        for t in range(tiles):
            for h in range(4):
                at = (h * 8 + m) * OWN
                row = pl.multiple_of((step * tiles + t) * 64, 64) + h * OWN
                out_ref[m, pl.ds(row, OWN), :] = sums[at : at + OWN, t * LANES : (t + 1) * LANES]


def middle_kernel(got_ref, out_ref):
    tiles = (got_ref.shape[1] - OWN) // 64

    def added(row):
        return sum(got_ref[m, row : row + OWN, :].astype(F32) for m in range(8))

    lane = lax.broadcasted_iota(jnp.int32, (OWN, LANES), 1)
    library = added(tiles * 64)
    for h in range(4):
        for t in range(tiles):
            out_ref[h, t * OWN : (t + 1) * OWN, :] = added(t * 64 + h * OWN).astype(BF16)
        mine = jnp.sum(jnp.where(lane // 4 == h, library, 0.0), axis=1, keepdims=True)
        out_ref[h, tiles * OWN :, :] = in_lanes(split3(mine), lane).astype(BF16)


def project_kernel(got_ref, loadings_ref, out_ref, rows_ref):
    tiles = got_ref.shape[1] // OWN - 1
    halves = loadings_ref.shape[1] // LANES

    def added(t):
        return sum(got_ref[h, t * OWN : (t + 1) * OWN, :].astype(F32) for h in range(4))

    library = jnp.sum(added(tiles), axis=1, keepdims=True)
    scores = jnp.zeros((OWN, loadings_ref.shape[1]), F32)
    rows_ref[...] = jnp.zeros_like(rows_ref)
    profile = []
    for t in range(tiles):
        normalized = jnp.log(1.0 + 10000.0 * added(t) / library).astype(BF16)
        rows_ref[pl.ds(t, OWN, stride=OWN), :] = normalized.astype(F32)
        profile.append(normalized)
    scores = jnp.dot(jnp.concatenate(profile, axis=1), loadings_ref[...], preferred_element_type=F32)
    for p, piece in enumerate(split3(scores)):
        for k in range(halves):
            at = tiles + p * halves + k
            rows_ref[pl.ds(at, OWN, stride=OWN), :] = piece[:, k * LANES : (k + 1) * LANES]
    for j in range(OWN):
        out_ref[j] = rows_ref[j * OWN : (j + 1) * OWN, :].astype(BF16)


def finish_kernel(got_ref, profile_ref, scores_ref):
    halves = scores_ref.shape[1] // LANES
    tiles = profile_ref.shape[1] // (got_ref.shape[0] * LANES)
    total = jnp.zeros((OWN, LANES), F32)
    for source in range(got_ref.shape[0]):
        block = got_ref[source].astype(F32)
        total += block
        for t in range(tiles):
            at = (source * tiles + t) * LANES
            profile_ref[:, at : at + LANES] = block[t : t + 1].astype(BF16)
    for k in range(halves):
        scores_ref[:, k * LANES : (k + 1) * LANES] = sum(
            total[tiles + p * halves + k : tiles + p * halves + k + 1] for p in range(3)
        )


def shards(labels, counts, library_size, loadings):
    cells, genes = counts.shape
    k = loadings.shape[1]
    tiles = genes // LANES
    width = 256
    sent = pl.pallas_call(
        sums_kernel,
        grid=(genes // width,),
        in_specs=[
            pl.BlockSpec((cells,), lambda i: (0,)),
            pl.BlockSpec((cells,), lambda i: (0,)),
            pl.BlockSpec((cells, width), lambda i: (0, i)),
        ],
        out_specs=pl.BlockSpec((8, tiles * 64 + OWN, LANES), lambda i: (0, 0, 0)),
        out_shape=jax.ShapeDtypeStruct((8, tiles * 64 + OWN, LANES), BF16),
        scratch_shapes=[pltpu.VMEM((G, cells), BF16)],
        compiler_params=pltpu.CompilerParams(vmem_limit_bytes=LIMIT),
    )(labels, library_size, counts)
    got = lax.all_to_all(sent, "dp", 0, 0, tiled=True, axis_index_groups=FIRST)
    sent = pl.pallas_call(
        middle_kernel,
        in_specs=[VMEM],
        out_specs=VMEM,
        out_shape=jax.ShapeDtypeStruct((4, tiles * OWN + OWN, LANES), BF16),
        compiler_params=pltpu.CompilerParams(vmem_limit_bytes=LIMIT),
    )(got)
    got = lax.all_to_all(sent, "dp", 0, 0, tiled=True, axis_index_groups=SECOND)
    sent = pl.pallas_call(
        project_kernel,
        in_specs=[VMEM, VMEM],
        out_specs=VMEM,
        out_shape=jax.ShapeDtypeStruct((16, OWN, LANES), BF16),
        scratch_shapes=[pltpu.VMEM((16 * OWN, LANES), F32)],
        compiler_params=pltpu.CompilerParams(vmem_limit_bytes=LIMIT),
    )(got, loadings)
    got = lax.all_to_all(sent, "gene", 0, 0, tiled=True)
    return pl.pallas_call(
        finish_kernel,
        in_specs=[VMEM],
        out_specs=(VMEM, VMEM),
        out_shape=(
            jax.ShapeDtypeStruct((1, 16 * genes), BF16),
            jax.ShapeDtypeStruct((1, k), F32),
        ),
        compiler_params=pltpu.CompilerParams(vmem_limit_bytes=LIMIT),
    )(got)


def solution(mesh):
    placed = (P("dp"), P("dp", "gene"), P("dp"), P("gene", None))
    return jax.shard_map(
        shards,
        mesh=mesh,
        in_specs=placed,
        out_specs=(P(("dp", "gene"), None), P(("dp", "gene"), None)),
        check_vma=False,
    )
```

time: 70.5 us -> 64.2 us (0.911)
  blocking collectives: 62.1 us -> 55.8 us
  Pallas kernels: 0 us -> 3.9 us
  matrix products: 3.65 us -> 0 us
  other arithmetic: 2.83 us -> 0 us
  local copies, waits for them, and re-layouts: 0.91 us -> 3.56 us
    all_to_all x2 -> x3, blocking collectives: 62.1 us -> 55.8 us  [the longest x1 21.9 us: shards(): got = lax.all_to_all(sent, 'gene', 0, 0, tiled=True)]
    pallas_call x0 -> x4, Pallas kernels: none -> 3.9 us  [the longest x1 2.77 us: shards(): pl.pallas_call(sums_kernel, grid=(genes // width,), in_specs=[pl.BlockSpe...]
    dot_general x2 -> x0, matrix products: 3.65 us -> none  [the longest x1 3.47 us: shards(): jnp.dot(members.astype(BF16), counts.astype(BF16), preferred_element_type...]
    unnamed x2 -> x8, local copies, waits for them, and re-layouts: 0.01 us -> 3.56 us
    reduce_sum x5 -> x0, other arithmetic: 1.86 us -> none  [the longest x1 0.98 us: shards(): jnp.sum(jnp.where(members, library_size.astype(F32)[None, :], 0.0), axis=1)]
    convert_element_type x4 -> x0, other arithmetic: 0.86 us -> none  [the longest x1 0.75 us: shards(): library_size.astype(F32)[None, :]]
    reshape x2 -> x0, local copies, waits for them, and re-layouts: 0.71 us -> none  [the longest x1 0.65 us: shards(): group_major = got[:, :rows].reshape(1, 16 * genes)]
where the time goes in v2:
time: 64.2 us; the launch traced here: 63.9 us
  blocking collectives  55.8 us (87%)
  Pallas kernels  3.9 us (6%)
  local copies, waits for them, and re-layouts  3.56 us (6%)
  between operations  0.66 us (1%)
    all_to_all x1, blocking collectives, shards(): got = lax.all_to_all(sent, 'gene', 0, 0, tiled=True)  21.9 us
    all_to_all x1, blocking collectives, shards(): got = lax.all_to_all(sent, 'dp', 0, 0, tiled=True, axis_index_groups=FIRST)  18.1 us
    all_to_all x1, blocking collectives, shards(): got = lax.all_to_all(sent, 'dp', 0, 0, tiled=True, axis_index_groups=SECOND)  15.8 us
    unnamed x8, local copies, waits for them, and re-layouts  3.56 us
    pallas_call x1, Pallas kernels, shards(): pl.pallas_call(sums_kernel, grid=(genes // width,), in_specs=[pl.BlockSpe...  2.77 us

profile of v2, /device:TPU:1, one launch (start us, length us, event | category | flops | bytes accessed | tf_op | source)
XLA Modules:
  0.0 63.9 jit_solution(9498038924225698429)
XLA Ops:
  0.6 0.0 copy-start
  0.6 2.2 %copy-done = s32[1024,1024]{1,0:T(8,128)S(1)} copy-done((s32[1024,1024]{1,0:T(8,128)S(1)}, s32[1024,1024]{1,0:T(8,128)}, u32[]{:S(2)}) %copy-start) | copy-done | bytes 4194328
  2.8 0.0 copy-start.2
  2.8 0.7 %copy-done.2 = s32[1024]{0:T(1024)S(1)} copy-done((s32[1024]{0:T(1024)S(1)}, s32[1024]{0:T(1024)}, u32[]{:S(2)}) %copy-start.2) | copy-done | bytes 4120
  3.5 0.0 copy-start.3
  3.5 0.7 %copy-done.3 = s32[1024]{0:T(1024)S(1)} copy-done((s32[1024]{0:T(1024)S(1)}, s32[1024]{0:T(1024)}, u32[]{:S(2)}) %copy-start.3) | copy-done | bytes 4120
  4.2 2.8 %shard_map.59 = bf16[8,528,128]{2,1,0:T(8,128)(2,1)S(1)} custom-call(s32[1024]{0:T(1024)S(1)} %copy-done.2, s32[1024]{0:T(1024)S(1)} %copy-done.3, s32[1024,1024]{1,0:T(8,128)S(1)} %copy-done), custom_call_target="tpu_custom_call" | custom-call | tf_op jit(solution)/shard_map/pallas_call | solution.py:127
  7.0 18.1 %all_to_all.15.got_ref = bf16[8,528,128]{2,1,0:T(8,128)(2,1)S(1)} all-to-all(bf16[8,528,128]{2,1,0:T(8,128)(2,1)S(1)} %shard_map.59), channel_id=1, replica_groups={{0,16,32,48,64,80,96,112},{128,144,160,176,192,208,224,240},{256,272,28..., dimensions={0} | all-to-all | bytes 2162688 | tf_op jit(solution)/shard_map/all_to_all | solution.py:140
  25.1 0.0 copy-start.1
  25.1 0.2 shard_map.60
  25.2 15.8 %all_to_all.16.got_ref = bf16[4,144,128]{2,1,0:T(8,128)(2,1)S(1)} all-to-all(bf16[4,144,128]{2,1,0:T(8,128)(2,1)S(1)} %shard_map.60), channel_id=1, replica_groups={{0,128,256,384},{16,144,272,400},{32,160,288,416},{48,176,304,432},{64,..., dimensions={0} | all-to-all | bytes 294912 | tf_op jit(solution)/shard_map/all_to_all | solution.py:148
  41.0 0.0 copy-done.1
  41.0 0.3 shard_map.61
  41.3 21.9 %all_to_all.17.got_ref = bf16[16,16,128]{2,1,0:T(8,128)(2,1)S(1)} all-to-all(bf16[16,16,128]{2,1,0:T(8,128)(2,1)S(1)} %shard_map.61), channel_id=1, replica_groups=mesh['dp'=32,'gene'=16] {'gene'}, dimensions={0} | all-to-all | bytes 131072 | tf_op jit(solution)/shard_map/all_to_all | solution.py:157
  63.2 0.7 %shard_map.62 = (bf16[1,16384]{1,0:T(2,128)(2,1)}, f32[1,256]{1,0:T(1,128)}) custom-call(bf16[16,16,128]{2,1,0:T(8,128)(2,1)S(1)} %all_to_all.17.got_ref), custom_call_target="tpu_custom_call" | custom-call | tf_op jit(solution)/shard_map/pallas_call | solution.py:158
Async XLA Ops:
  0.6 2.2 %copy-start = (s32[1024,1024]{1,0:T(8,128)S(1)}, s32[1024,1024]{1,0:T(8,128)}, u32[]{:S(2)}) copy-start(s32[1024,1024]{1,0:T(8,128)} %counts_ref.1) | copy-start | bytes 12582916
  2.8 0.7 %copy-start.2 = (s32[1024]{0:T(1024)S(1)}, s32[1024]{0:T(1024)}, u32[]{:S(2)}) copy-start(s32[1024]{0:T(1024)} %labels_ref.1) | copy-start | bytes 12292
  3.5 0.7 %copy-start.3 = (s32[1024]{0:T(1024)S(1)}, s32[1024]{0:T(1024)}, u32[]{:S(2)}) copy-start(s32[1024]{0:T(1024)} %lib_ref.1) | copy-start | bytes 12292
  25.1 15.9 %copy-start.1 = (bf16[1024,256]{1,0:T(8,128)(2,1)S(1)}, bf16[1024,256]{1,0:T(8,128)(2,1)}, u32[]{:S(2)}) copy-start(bf16[1024,256]{1,0:T(8,128)(2,1)} %loadings_ref.1) | copy-start | bytes 1572868

commit v3 on v2

--- a/solution.py
+++ b/solution.py
@@ -10,9 +10,11 @@
 BF16 = jnp.bfloat16
 LANES = 128
 OWN = 16
-FIRST = [[(2 * h + l) * 4 + x for l in range(2) for x in range(4)] for h in range(4)]
-SECOND = [[(2 * h + l) * 4 + x for h in range(4)] for l in range(2) for x in range(4)]
+SETS = ((1, 2, 4, 7), (0, 3, 5, 6))
+FIRST = [[y[h] * 4 + x for y in SETS for x in range(4)] for h in range(4)]
+SECOND = [[y[h] * 4 + x for h in range(4)] for y in SETS for x in range(4)]
 VMEM = pl.BlockSpec(memory_space=pltpu.VMEM)
+HBM = pl.BlockSpec(memory_space=pltpu.HBM)
 LIMIT = 48 * 1024 * 1024
 
 
@@ -26,42 +28,71 @@
     return jnp.where(lane == 0, pieces[0], jnp.where(lane == 1, pieces[1], jnp.where(lane == 2, pieces[2], 0.0)))
 
 
-def sums_kernel(labels_ref, lib_ref, counts_ref, out_ref, members_ref):
-    step = pl.program_id(0)
-    cells = counts_ref.shape[0]
-    width = counts_ref.shape[1]
+def sums_kernel(
+    labels_hbm,
+    lib_hbm,
+    counts_hbm,
+    out_ref,
+    labels_ref,
+    lib_ref,
+    counts_ref,
+    members_ref,
+    part_ref,
+    tile_ref,
+    small_sems,
+    sems,
+):
+    blocks, cells, width = counts_ref.shape
     tiles = width // LANES
-
-    @pl.when(step == 0)
-    def _():
-        group = lax.broadcasted_iota(jnp.int32, (G, cells), 0)
-        members_ref[...] = (group == labels_ref[...].reshape(1, cells)).astype(F32).astype(BF16)
-        size = lib_ref[...].reshape(1, cells)
-        high = size // 256
-        low = size - high * 256
-        part = jnp.where(lax.broadcasted_iota(jnp.int32, (2 * LANES, cells), 0) < LANES, high, low)
-        both = lax.dot_general(
-            members_ref[...], part.astype(F32).astype(BF16), (((1,), (1,)), ((), ())), preferred_element_type=F32
-        )
-        total = both[:, :LANES] * 256.0 + both[:, LANES:]
-        lane = lax.broadcasted_iota(jnp.int32, (G, LANES), 1)
-        placed = in_lanes(split3(total), lane % 4)
-        lane = lax.broadcasted_iota(jnp.int32, (OWN, LANES), 1) // 4
-        for m in range(8):
-            tile = jnp.zeros((OWN, LANES), F32)
-            for h in range(4):
-                at = (h * 8 + m) * OWN
-                tile = jnp.where(lane == h, placed[at : at + OWN], tile)
-            out_ref[m, out_ref.shape[1] - OWN :, :] = tile.astype(BF16)
-
-    sums = jnp.dot(members_ref[...], counts_ref[...].astype(F32).astype(BF16), preferred_element_type=F32)
-    sums = sums.astype(BF16)
-    for m in range(8):
+    span = tiles * 64
+    chunk = G // 4
+    end = blocks * span
+
+    def arriving(b):
+        columns = pl.ds(pl.multiple_of(b * width, width), width)
+        return pltpu.make_async_copy(counts_hbm.at[:, columns], counts_ref.at[b], sems.at[b])
+
+    labels_copy = pltpu.make_async_copy(labels_hbm, labels_ref, small_sems.at[0])
+    lib_copy = pltpu.make_async_copy(lib_hbm, lib_ref, small_sems.at[1])
+    labels_copy.start()
+    lib_copy.start()
+
+    @pl.loop(0, blocks)
+    def _(b):
+        arriving(b).start()
+
+    tile_ref[...] = jnp.zeros_like(tile_ref)
+    labels_copy.wait()
+    lib_copy.wait()
+    size = lib_ref[...].reshape(1, cells)
+    high = size // 256
+    part_ref[:LANES] = jnp.broadcast_to(high.astype(F32), (LANES, cells)).astype(BF16)
+    part_ref[LANES:] = jnp.broadcast_to((size - high * 256).astype(F32), (LANES, cells)).astype(BF16)
+
+    @pl.loop(0, 4)
+    def _(h):
+        at = pl.multiple_of(h * chunk, chunk)
+        swap = jnp.where((h == 0) | (h == 3), chunk // 2, 0)
+        group = (lax.broadcasted_iota(jnp.int32, (chunk, cells), 0) ^ swap) + at
+        members = (group == labels_ref[...].reshape(1, cells)).astype(F32).astype(BF16)
+        members_ref[pl.ds(at, chunk), :] = members
+        both = lax.dot_general(members, part_ref[...], (((1,), (1,)), ((), ())), preferred_element_type=F32)
+        lane = lax.broadcasted_iota(jnp.int32, (chunk, LANES), 1)
+        placed = in_lanes(split3(both[:, :LANES] * 256.0 + both[:, LANES:]), lane % 4)
+        tile_ref[...] = jnp.where(lane // 4 == h, placed, tile_ref[...])
+
+    out_ref[:, end:, :] = tile_ref[...].astype(BF16).reshape(8, OWN, LANES)
+
+    @pl.loop(0, blocks)
+    def _(b):
+        arriving(b).wait()
+        sums = jnp.dot(members_ref[...], counts_ref[b].astype(F32).astype(BF16), preferred_element_type=F32)
+        sums = sums.astype(BF16)
         for t in range(tiles):
             for h in range(4):
-                at = (h * 8 + m) * OWN
-                row = pl.multiple_of((step * tiles + t) * 64, 64) + h * OWN
-                out_ref[m, pl.ds(row, OWN), :] = sums[at : at + OWN, t * LANES : (t + 1) * LANES]
+                row = pl.multiple_of(b * span, span) + t * 64 + h * OWN
+                part = sums[h * chunk : (h + 1) * chunk, t * LANES : (t + 1) * LANES]
+                out_ref[:, pl.ds(row, OWN), :] = part.reshape(8, OWN, LANES)
 
 
 def middle_kernel(got_ref, out_ref):
@@ -123,20 +154,24 @@
     cells, genes = counts.shape
     k = loadings.shape[1]
     tiles = genes // LANES
-    width = 256
+    width = 512
     sent = pl.pallas_call(
         sums_kernel,
-        grid=(genes // width,),
-        in_specs=[
-            pl.BlockSpec((cells,), lambda i: (0,)),
-            pl.BlockSpec((cells,), lambda i: (0,)),
-            pl.BlockSpec((cells, width), lambda i: (0, i)),
+        in_specs=[HBM, HBM, HBM],
+        out_specs=VMEM,
+        out_shape=pltpu.VMEM((8, tiles * 64 + OWN, LANES), BF16),
+        scratch_shapes=[
+            pltpu.VMEM((cells,), jnp.int32),
+            pltpu.VMEM((cells,), jnp.int32),
+            pltpu.VMEM((genes // width, cells, width), jnp.int32),
+            pltpu.VMEM((G, cells), BF16),
+            pltpu.VMEM((2 * LANES, cells), BF16),
+            pltpu.VMEM((LANES, LANES), F32),
+            pltpu.SemaphoreType.DMA((2,)),
+            pltpu.SemaphoreType.DMA((genes // width,)),
         ],
-        out_specs=pl.BlockSpec((8, tiles * 64 + OWN, LANES), lambda i: (0, 0, 0)),
-        out_shape=jax.ShapeDtypeStruct((8, tiles * 64 + OWN, LANES), BF16),
-        scratch_shapes=[pltpu.VMEM((G, cells), BF16)],
-        compiler_params=pltpu.CompilerParams(vmem_limit_bytes=LIMIT),
-    )(labels, library_size, counts)
+        compiler_params=pltpu.CompilerParams(vmem_limit_bytes=LIMIT),
+    )(*(pltpu.with_memory_space_constraint(array, pltpu.HBM) for array in (labels, library_size, counts)))
     got = lax.all_to_all(sent, "dp", 0, 0, tiled=True, axis_index_groups=FIRST)
     sent = pl.pallas_call(
         middle_kernel,

time: 64.2 us -> 59.3 us (0.924)
  local copies, waits for them, and re-layouts: 3.56 us -> 0.01 us
  blocking collectives: 55.8 us -> 53.6 us
  Pallas kernels: 3.9 us -> 4.87 us
    unnamed x8 -> x2, local copies, waits for them, and re-layouts: 3.56 us -> 0.01 us
    all_to_all x1, blocking collectives: 18.1 us -> 17 us  [shards(): got = lax.all_to_all(sent, 'dp', 0, 0, tiled=True, axis_index_groups=FIRST)]
    pallas_call x1, Pallas kernels: 2.77 us -> 3.74 us  [shards(): pl.pallas_call(sums_kernel, in_specs=[HBM, HBM, HBM], out_specs=VMEM, out...]
    all_to_all x1, blocking collectives: 15.8 us -> 15 us  [shards(): got = lax.all_to_all(sent, 'dp', 0, 0, tiled=True, axis_index_groups=SECOND)]
where the time goes in v3:
time: 59.3 us; the launch traced here: 59.1 us
  blocking collectives  53.6 us (90%)
  Pallas kernels  4.87 us (8%)
  between operations  0.65 us (1%)
    all_to_all x1, blocking collectives, shards(): got = lax.all_to_all(sent, 'gene', 0, 0, tiled=True)  21.6 us
    all_to_all x1, blocking collectives, shards(): got = lax.all_to_all(sent, 'dp', 0, 0, tiled=True, axis_index_groups=FIRST)  17 us
    all_to_all x1, blocking collectives, shards(): got = lax.all_to_all(sent, 'dp', 0, 0, tiled=True, axis_index_groups=SECOND)  15 us
    pallas_call x1, Pallas kernels, shards(): pl.pallas_call(sums_kernel, in_specs=[HBM, HBM, HBM], out_specs=VMEM, out...  3.74 us

profile of v3, /device:TPU:1, one launch (start us, length us, event | category | flops | bytes accessed | tf_op | source)
XLA Modules:
  0.0 59.1 jit_solution(1825491971299179385)
XLA Ops:
  0.6 3.7 %shard_map.59 = bf16[8,528,128]{2,1,0:T(8,128)(2,1)S(1)} custom-call(s32[1024]{0:T(1024)} %labels_hbm.1, s32[1024]{0:T(1024)} %lib_hbm.1, s32[1024,1024]{1,0:T(8,128)} %counts_hbm.1), custom_call_target="tpu_custom_call" | custom-call | tf_op jit(solution)/shard_map/pallas_call | solution.py:158
  4.4 17.0 %all_to_all.15.got_ref = bf16[8,528,128]{2,1,0:T(8,128)(2,1)S(1)} all-to-all(bf16[8,528,128]{2,1,0:T(8,128)(2,1)S(1)} %shard_map.59), channel_id=1, replica_groups={{64,80,96,112,0,16,32,48},{128,144,160,176,192,208,224,240},{256,272,28..., dimensions={0} | all-to-all | bytes 2162688 | tf_op jit(solution)/shard_map/all_to_all | solution.py:175
  21.3 0.0 copy-start
  21.3 0.2 shard_map.60
  21.5 15.0 %all_to_all.16.got_ref = bf16[4,144,128]{2,1,0:T(8,128)(2,1)S(1)} all-to-all(bf16[4,144,128]{2,1,0:T(8,128)(2,1)S(1)} %shard_map.60), channel_id=1, replica_groups={{64,128,256,448},{80,144,272,464},{96,160,288,480},{112,176,304,496},{0..., dimensions={0} | all-to-all | bytes 294912 | tf_op jit(solution)/shard_map/all_to_all | solution.py:183
  36.6 0.0 copy-done
  36.6 0.3 shard_map.61
  36.8 21.6 %all_to_all.17.got_ref = bf16[16,16,128]{2,1,0:T(8,128)(2,1)S(1)} all-to-all(bf16[16,16,128]{2,1,0:T(8,128)(2,1)S(1)} %shard_map.61), channel_id=1, replica_groups=mesh['dp'=32,'gene'=16] {'gene'}, dimensions={0} | all-to-all | bytes 131072 | tf_op jit(solution)/shard_map/all_to_all | solution.py:192
  58.4 0.7 %shard_map.62 = (bf16[1,16384]{1,0:T(2,128)(2,1)}, f32[1,256]{1,0:T(1,128)}) custom-call(bf16[16,16,128]{2,1,0:T(8,128)(2,1)S(1)} %all_to_all.17.got_ref), custom_call_target="tpu_custom_call" | custom-call | tf_op jit(solution)/shard_map/pallas_call | solution.py:193
Async XLA Ops:
  21.3 15.2 %copy-start = (bf16[1024,256]{1,0:T(8,128)(2,1)S(1)}, bf16[1024,256]{1,0:T(8,128)(2,1)}, u32[]{:S(2)}) copy-start(bf16[1024,256]{1,0:T(8,128)(2,1)} %loadings_ref.1) | copy-start | bytes 1572868

commit v4 on v3

--- a/solution.py
+++ b/solution.py
@@ -10,9 +10,29 @@
 BF16 = jnp.bfloat16
 LANES = 128
 OWN = 16
-SETS = ((1, 2, 4, 7), (0, 3, 5, 6))
-FIRST = [[y[h] * 4 + x for y in SETS for x in range(4)] for h in range(4)]
-SECOND = [[y[h] * 4 + x for h in range(4)] for y in SETS for x in range(4)]
+Y_SETS = ((1, 2, 4, 7), (0, 3, 5, 6))
+X_SETS = ((1, 2), (0, 3))
+TILE, TILES = 4, 8
+
+
+def member(z, core, y, x):
+    return ((y + core) % 8 * 4 + (x + core) % 4) * 16 + z * 2 + core
+
+
+FIRST = [
+    [member(z, core, ys[h], xs[q]) for ys in Y_SETS for xs in X_SETS]
+    for z in range(8)
+    for core in range(2)
+    for h in range(4)
+    for q in range(2)
+]
+SECOND = [
+    [member(z, core, ys[h], xs[q]) for h in range(4) for q in range(2)]
+    for z in range(8)
+    for core in range(2)
+    for ys in Y_SETS
+    for xs in X_SETS
+]
 VMEM = pl.BlockSpec(memory_space=pltpu.VMEM)
 HBM = pl.BlockSpec(memory_space=pltpu.HBM)
 LIMIT = 48 * 1024 * 1024
@@ -26,6 +46,15 @@
 
 def in_lanes(pieces, lane):
     return jnp.where(lane == 0, pieces[0], jnp.where(lane == 1, pieces[1], jnp.where(lane == 2, pieces[2], 0.0)))
+
+
+def row_of(group, core):
+    y = ((group >> 6) - core) & 7
+    x = ((group >> 4) - core) & 3
+    h, q = y >> 1, x >> 1
+    y_set = (y ^ h ^ (h >> 1) ^ 1) & 1
+    x_set = (x ^ q ^ 1) & 1
+    return (((h * 2 + q) * 2 + y_set) * 2 + x_set) * OWN + (group & (OWN - 1))
 
 
 def sums_kernel(
@@ -37,6 +66,7 @@
     lib_ref,
     counts_ref,
     members_ref,
+    rows_ref,
     part_ref,
     tile_ref,
     small_sems,
@@ -44,8 +74,10 @@
 ):
     blocks, cells, width = counts_ref.shape
     tiles = width // LANES
-    span = tiles * 64
-    chunk = G // 4
+    span = tiles * TILES * OWN
+    part = TILE * OWN
+    chunk = 2 * part
+    core = lax.axis_index("gene") & 1
     end = blocks * span
 
     def arriving(b):
@@ -64,24 +96,26 @@
     tile_ref[...] = jnp.zeros_like(tile_ref)
     labels_copy.wait()
     lib_copy.wait()
+    rows_ref[...] = row_of(labels_ref[...].reshape(1, cells), core)
     size = lib_ref[...].reshape(1, cells)
     high = size // 256
     part_ref[:LANES] = jnp.broadcast_to(high.astype(F32), (LANES, cells)).astype(BF16)
     part_ref[LANES:] = jnp.broadcast_to((size - high * 256).astype(F32), (LANES, cells)).astype(BF16)
 
-    @pl.loop(0, 4)
-    def _(h):
-        at = pl.multiple_of(h * chunk, chunk)
-        swap = jnp.where((h == 0) | (h == 3), chunk // 2, 0)
-        group = (lax.broadcasted_iota(jnp.int32, (chunk, cells), 0) ^ swap) + at
-        members = (group == labels_ref[...].reshape(1, cells)).astype(F32).astype(BF16)
+    @pl.loop(0, G // chunk)
+    def _(i):
+        at = pl.multiple_of(i * chunk, chunk)
+        row = lax.broadcasted_iota(jnp.int32, (chunk, cells), 0) + at
+        members = (row == rows_ref[...]).astype(F32).astype(BF16)
         members_ref[pl.ds(at, chunk), :] = members
         both = lax.dot_general(members, part_ref[...], (((1,), (1,)), ((), ())), preferred_element_type=F32)
         lane = lax.broadcasted_iota(jnp.int32, (chunk, LANES), 1)
         placed = in_lanes(split3(both[:, :LANES] * 256.0 + both[:, LANES:]), lane % 4)
-        tile_ref[...] = jnp.where(lane // 4 == h, placed, tile_ref[...])
-
-    out_ref[:, end:, :] = tile_ref[...].astype(BF16).reshape(8, OWN, LANES)
+        lane = lax.broadcasted_iota(jnp.int32, (part, LANES), 1) // 4
+        tile = jnp.where(lane == 2 * i, placed[:part], tile_ref[...])
+        tile_ref[...] = jnp.where(lane == 2 * i + 1, placed[part:], tile)
+
+    out_ref[:, end:, :] = tile_ref[...].astype(BF16).reshape(TILE, OWN, LANES)
 
     @pl.loop(0, blocks)
     def _(b):
@@ -89,23 +123,23 @@
         sums = jnp.dot(members_ref[...], counts_ref[b].astype(F32).astype(BF16), preferred_element_type=F32)
         sums = sums.astype(BF16)
         for t in range(tiles):
-            for h in range(4):
-                row = pl.multiple_of(b * span, span) + t * 64 + h * OWN
-                part = sums[h * chunk : (h + 1) * chunk, t * LANES : (t + 1) * LANES]
-                out_ref[:, pl.ds(row, OWN), :] = part.reshape(8, OWN, LANES)
+            for h in range(TILES):
+                row = pl.multiple_of(b * span, span) + (t * TILES + h) * OWN
+                block = sums[h * part : (h + 1) * part, t * LANES : (t + 1) * LANES]
+                out_ref[:, pl.ds(row, OWN), :] = block.reshape(TILE, OWN, LANES)
 
 
 def middle_kernel(got_ref, out_ref):
-    tiles = (got_ref.shape[1] - OWN) // 64
+    tiles = (got_ref.shape[1] - OWN) // (TILES * OWN)
 
     def added(row):
-        return sum(got_ref[m, row : row + OWN, :].astype(F32) for m in range(8))
+        return sum(got_ref[m, row : row + OWN, :].astype(F32) for m in range(TILE))
 
     lane = lax.broadcasted_iota(jnp.int32, (OWN, LANES), 1)
-    library = added(tiles * 64)
-    for h in range(4):
+    library = added(tiles * TILES * OWN)
+    for h in range(TILES):
         for t in range(tiles):
-            out_ref[h, t * OWN : (t + 1) * OWN, :] = added(t * 64 + h * OWN).astype(BF16)
+            out_ref[h, t * OWN : (t + 1) * OWN, :] = added((t * TILES + h) * OWN).astype(BF16)
         mine = jnp.sum(jnp.where(lane // 4 == h, library, 0.0), axis=1, keepdims=True)
         out_ref[h, tiles * OWN :, :] = in_lanes(split3(mine), lane).astype(BF16)
 
@@ -115,7 +149,7 @@
     halves = loadings_ref.shape[1] // LANES
 
     def added(t):
-        return sum(got_ref[h, t * OWN : (t + 1) * OWN, :].astype(F32) for h in range(4))
+        return sum(got_ref[h, t * OWN : (t + 1) * OWN, :].astype(F32) for h in range(TILES))
 
     library = jnp.sum(added(tiles), axis=1, keepdims=True)
     scores = jnp.zeros((OWN, loadings_ref.shape[1]), F32)
@@ -159,28 +193,29 @@
         sums_kernel,
         in_specs=[HBM, HBM, HBM],
         out_specs=VMEM,
-        out_shape=pltpu.VMEM((8, tiles * 64 + OWN, LANES), BF16),
+        out_shape=pltpu.VMEM((TILE, tiles * TILES * OWN + OWN, LANES), BF16),
         scratch_shapes=[
             pltpu.VMEM((cells,), jnp.int32),
             pltpu.VMEM((cells,), jnp.int32),
             pltpu.VMEM((genes // width, cells, width), jnp.int32),
             pltpu.VMEM((G, cells), BF16),
+            pltpu.VMEM((1, cells), jnp.int32),
             pltpu.VMEM((2 * LANES, cells), BF16),
-            pltpu.VMEM((LANES, LANES), F32),
+            pltpu.VMEM((TILE * OWN, LANES), F32),
             pltpu.SemaphoreType.DMA((2,)),
             pltpu.SemaphoreType.DMA((genes // width,)),
         ],
         compiler_params=pltpu.CompilerParams(vmem_limit_bytes=LIMIT),
     )(*(pltpu.with_memory_space_constraint(array, pltpu.HBM) for array in (labels, library_size, counts)))
-    got = lax.all_to_all(sent, "dp", 0, 0, tiled=True, axis_index_groups=FIRST)
+    got = lax.all_to_all(sent, ("dp", "gene"), 0, 0, tiled=True, axis_index_groups=FIRST)
     sent = pl.pallas_call(
         middle_kernel,
         in_specs=[VMEM],
         out_specs=VMEM,
-        out_shape=jax.ShapeDtypeStruct((4, tiles * OWN + OWN, LANES), BF16),
+        out_shape=jax.ShapeDtypeStruct((TILES, tiles * OWN + OWN, LANES), BF16),
         compiler_params=pltpu.CompilerParams(vmem_limit_bytes=LIMIT),
     )(got)
-    got = lax.all_to_all(sent, "dp", 0, 0, tiled=True, axis_index_groups=SECOND)
+    got = lax.all_to_all(sent, ("dp", "gene"), 0, 0, tiled=True, axis_index_groups=SECOND)
     sent = pl.pallas_call(
         project_kernel,
         in_specs=[VMEM, VMEM],

time: 59.3 us -> 58.1 us (0.980)
  blocking collectives: 53.6 us -> 52.4 us
    all_to_all x2, blocking collectives: 32 us -> 27 us  [shards(): lax.all_to_all(sent, ('dp', 'gene'), 0, 0, tiled=True, axis_index_groups=...]
    all_to_all x1, blocking collectives: 21.6 us -> 25.4 us  [shards(): got = lax.all_to_all(sent, 'gene', 0, 0, tiled=True)]
where the time goes in v4:
time: 58.1 us; the launch traced here: 57.9 us
  blocking collectives  52.4 us (90%)
  Pallas kernels  4.86 us (8%)
  between operations  0.65 us (1%)
    all_to_all x2, blocking collectives, shards(): lax.all_to_all(sent, ('dp', 'gene'), 0, 0, tiled=True, axis_index_groups=...  27 us
    all_to_all x1, blocking collectives, shards(): got = lax.all_to_all(sent, 'gene', 0, 0, tiled=True)  25.4 us
    pallas_call x1, Pallas kernels, shards(): pl.pallas_call(sums_kernel, in_specs=[HBM, HBM, HBM], out_specs=VMEM, out...  3.73 us

profile of v4, /device:TPU:1, one launch (start us, length us, event | category | flops | bytes accessed | tf_op | source)
XLA Modules:
  0.0 57.9 jit_solution(17360962249179835905)
XLA Ops:
  0.6 3.7 %shard_map.59 = bf16[4,1040,128]{2,1,0:T(8,128)(2,1)S(1)} custom-call(s32[1024]{0:T(1024)} %labels_hbm.1, s32[1024]{0:T(1024)} %lib_hbm.1, s32[1024,1024]{1,0:T(8,128)} %counts_hbm.1), custom_call_target="tpu_custom_call" | custom-call | tf_op jit(solution)/shard_map/pallas_call | solution.py:192
  4.4 16.8 %all_to_all.15.got_ref = bf16[4,1040,128]{2,1,0:T(8,128)(2,1)S(1)} all-to-all(bf16[4,1040,128]{2,1,0:T(8,128)(2,1)S(1)} %shard_map.59), channel_id=1, replica_groups={{80,64,16,0},{96,112,32,48},{144,128,208,192},{160,176,224,240},{272,25..., dimensions={0} | all-to-all | bytes 2129920 | tf_op jit(solution)/shard_map/all_to_all | solution.py:210
  21.2 0.0 copy-start
  21.2 0.2 shard_map.60
  21.4 10.2 %all_to_all.16.got_ref = bf16[8,144,128]{2,1,0:T(8,128)(2,1)S(1)} all-to-all(bf16[8,144,128]{2,1,0:T(8,128)(2,1)S(1)} %shard_map.60), channel_id=1, replica_groups={{80,96,144,160,272,288,464,480},{64,112,128,176,256,304,448,496},{16,32..., dimensions={0} | all-to-all | bytes 589824 | tf_op jit(solution)/shard_map/all_to_all | solution.py:218
  31.5 0.0 copy-done
  31.5 0.3 shard_map.61
  31.8 25.4 %all_to_all.17.got_ref = bf16[16,16,128]{2,1,0:T(8,128)(2,1)S(1)} all-to-all(bf16[16,16,128]{2,1,0:T(8,128)(2,1)S(1)} %shard_map.61), channel_id=1, replica_groups=mesh['dp'=32,'gene'=16] {'gene'}, dimensions={0} | all-to-all | bytes 131072 | tf_op jit(solution)/shard_map/all_to_all | solution.py:227
  57.2 0.7 %shard_map.62 = (bf16[1,16384]{1,0:T(2,128)(2,1)}, f32[1,256]{1,0:T(1,128)}) custom-call(bf16[16,16,128]{2,1,0:T(8,128)(2,1)S(1)} %all_to_all.17.got_ref), custom_call_target="tpu_custom_call" | custom-call | tf_op jit(solution)/shard_map/pallas_call | solution.py:228
Async XLA Ops:
  21.2 10.3 %copy-start = (bf16[1024,256]{1,0:T(8,128)(2,1)S(1)}, bf16[1024,256]{1,0:T(8,128)(2,1)}, u32[]{:S(2)}) copy-start(bf16[1024,256]{1,0:T(8,128)(2,1)} %loadings_ref.1) | copy-start | bytes 1572868

commit v5 on v4

--- a/solution.py
+++ b/solution.py
@@ -67,8 +67,6 @@
     counts_ref,
     members_ref,
     rows_ref,
-    part_ref,
-    tile_ref,
     small_sems,
     sems,
 ):
@@ -93,29 +91,27 @@
     def _(b):
         arriving(b).start()
 
-    tile_ref[...] = jnp.zeros_like(tile_ref)
     labels_copy.wait()
-    lib_copy.wait()
     rows_ref[...] = row_of(labels_ref[...].reshape(1, cells), core)
-    size = lib_ref[...].reshape(1, cells)
-    high = size // 256
-    part_ref[:LANES] = jnp.broadcast_to(high.astype(F32), (LANES, cells)).astype(BF16)
-    part_ref[LANES:] = jnp.broadcast_to((size - high * 256).astype(F32), (LANES, cells)).astype(BF16)
 
     @pl.loop(0, G // chunk)
     def _(i):
         at = pl.multiple_of(i * chunk, chunk)
         row = lax.broadcasted_iota(jnp.int32, (chunk, cells), 0) + at
-        members = (row == rows_ref[...]).astype(F32).astype(BF16)
-        members_ref[pl.ds(at, chunk), :] = members
-        both = lax.dot_general(members, part_ref[...], (((1,), (1,)), ((), ())), preferred_element_type=F32)
-        lane = lax.broadcasted_iota(jnp.int32, (chunk, LANES), 1)
-        placed = in_lanes(split3(both[:, :LANES] * 256.0 + both[:, LANES:]), lane % 4)
-        lane = lax.broadcasted_iota(jnp.int32, (part, LANES), 1) // 4
-        tile = jnp.where(lane == 2 * i, placed[:part], tile_ref[...])
-        tile_ref[...] = jnp.where(lane == 2 * i + 1, placed[part:], tile)
-
-    out_ref[:, end:, :] = tile_ref[...].astype(BF16).reshape(TILE, OWN, LANES)
+        members_ref[pl.ds(at, chunk), :] = (row == rows_ref[...]).astype(F32).astype(BF16)
+
+    lib_copy.wait()
+    size = lib_ref[...].reshape(1, cells)
+    low = size & 255
+    lane = lax.broadcasted_iota(jnp.int32, (LANES, cells), 0)
+    sizes = jnp.where(lane & 4 == 0, size - low, low).astype(F32).astype(BF16)
+    total = lax.dot_general(members_ref[...], sizes, (((1,), (1,)), ((), ())), preferred_element_type=F32)
+    placed = in_lanes(split3(total), lax.broadcasted_iota(jnp.int32, (G, LANES), 1) & 3)
+    lane = lax.broadcasted_iota(jnp.int32, (part, LANES), 1) >> 3
+    tile = jnp.zeros((part, LANES), F32)
+    for h in range(TILES):
+        tile = jnp.where(lane == h, placed[h * part : (h + 1) * part], tile)
+    out_ref[:, end:, :] = tile.astype(BF16).reshape(TILE, OWN, LANES)
 
     @pl.loop(0, blocks)
     def _(b):
@@ -140,7 +136,7 @@
     for h in range(TILES):
         for t in range(tiles):
             out_ref[h, t * OWN : (t + 1) * OWN, :] = added((t * TILES + h) * OWN).astype(BF16)
-        mine = jnp.sum(jnp.where(lane // 4 == h, library, 0.0), axis=1, keepdims=True)
+        mine = jnp.sum(jnp.where(lane >> 3 == h, library, 0.0), axis=1, keepdims=True)
         out_ref[h, tiles * OWN :, :] = in_lanes(split3(mine), lane).astype(BF16)
 
 
@@ -152,7 +148,6 @@
         return sum(got_ref[h, t * OWN : (t + 1) * OWN, :].astype(F32) for h in range(TILES))
 
     library = jnp.sum(added(tiles), axis=1, keepdims=True)
-    scores = jnp.zeros((OWN, loadings_ref.shape[1]), F32)
     rows_ref[...] = jnp.zeros_like(rows_ref)
     profile = []
     for t in range(tiles):
@@ -184,12 +179,11 @@
         )
 
 
-def shards(labels, counts, library_size, loadings):
+def local_sums(labels, library_size, counts):
     cells, genes = counts.shape
-    k = loadings.shape[1]
     tiles = genes // LANES
     width = 512
-    sent = pl.pallas_call(
+    return pl.pallas_call(
         sums_kernel,
         in_specs=[HBM, HBM, HBM],
         out_specs=VMEM,
@@ -200,13 +194,18 @@
             pltpu.VMEM((genes // width, cells, width), jnp.int32),
             pltpu.VMEM((G, cells), BF16),
             pltpu.VMEM((1, cells), jnp.int32),
-            pltpu.VMEM((2 * LANES, cells), BF16),
-            pltpu.VMEM((TILE * OWN, LANES), F32),
             pltpu.SemaphoreType.DMA((2,)),
             pltpu.SemaphoreType.DMA((genes // width,)),
         ],
         compiler_params=pltpu.CompilerParams(vmem_limit_bytes=LIMIT),
     )(*(pltpu.with_memory_space_constraint(array, pltpu.HBM) for array in (labels, library_size, counts)))
+
+
+def shards(labels, counts, library_size, loadings):
+    cells, genes = counts.shape
+    k = loadings.shape[1]
+    tiles = genes // LANES
+    sent = local_sums(labels, library_size, counts)
     got = lax.all_to_all(sent, ("dp", "gene"), 0, 0, tiled=True, axis_index_groups=FIRST)
     sent = pl.pallas_call(
         middle_kernel,

time: 58.1 us -> 57.5 us (0.990)
  no operation moved by 1% of the time
where the time goes in v5:
time: 57.5 us; the launch traced here: 57.3 us
  blocking collectives  52.4 us (91%)
  Pallas kernels  4.31 us (7%)
  between operations  0.65 us (1%)
    all_to_all x2, blocking collectives, shards(): lax.all_to_all(sent, ('dp', 'gene'), 0, 0, tiled=True, axis_index_groups=...  27 us
    all_to_all x1, blocking collectives, shards(): got = lax.all_to_all(sent, 'gene', 0, 0, tiled=True)  25.4 us
    pallas_call x1, Pallas kernels, local_sums(): pl.pallas_call(sums_kernel, in_specs=[HBM, HBM, HBM], out_specs=VMEM, out...  3.19 us

profile of v5, /device:TPU:1, one launch (start us, length us, event | category | flops | bytes accessed | tf_op | source)
XLA Modules:
  0.0 57.3 jit_solution(12753141828434958736)
XLA Ops:
  0.6 3.2 %shard_map.59 = bf16[4,1040,128]{2,1,0:T(8,128)(2,1)S(1)} custom-call(s32[1024]{0:T(1024)} %labels_hbm.1, s32[1024]{0:T(1024)} %lib_hbm.1, s32[1024,1024]{1,0:T(8,128)} %counts_hbm.1), custom_call_target="tpu_custom_call" | custom-call | tf_op jit(solution)/shard_map/pallas_call | solution.py:186
  3.8 16.8 %all_to_all.15.got_ref = bf16[4,1040,128]{2,1,0:T(8,128)(2,1)S(1)} all-to-all(bf16[4,1040,128]{2,1,0:T(8,128)(2,1)S(1)} %shard_map.59), channel_id=1, replica_groups={{80,64,16,0},{96,112,32,48},{144,128,208,192},{160,176,224,240},{272,25..., dimensions={0} | all-to-all | bytes 2129920 | tf_op jit(solution)/shard_map/all_to_all | solution.py:209
  20.7 0.0 copy-start
  20.7 0.2 shard_map.60
  20.8 10.2 %all_to_all.16.got_ref = bf16[8,144,128]{2,1,0:T(8,128)(2,1)S(1)} all-to-all(bf16[8,144,128]{2,1,0:T(8,128)(2,1)S(1)} %shard_map.60), channel_id=1, replica_groups={{80,96,144,160,272,288,464,480},{64,112,128,176,256,304,448,496},{16,32..., dimensions={0} | all-to-all | bytes 589824 | tf_op jit(solution)/shard_map/all_to_all | solution.py:217
  31.0 0.0 copy-done
  31.0 0.3 shard_map.61
  31.3 25.4 %all_to_all.17.got_ref = bf16[16,16,128]{2,1,0:T(8,128)(2,1)S(1)} all-to-all(bf16[16,16,128]{2,1,0:T(8,128)(2,1)S(1)} %shard_map.61), channel_id=1, replica_groups=mesh['dp'=32,'gene'=16] {'gene'}, dimensions={0} | all-to-all | bytes 131072 | tf_op jit(solution)/shard_map/all_to_all | solution.py:226
  56.6 0.7 %shard_map.62 = (bf16[1,16384]{1,0:T(2,128)(2,1)}, f32[1,256]{1,0:T(1,128)}) custom-call(bf16[16,16,128]{2,1,0:T(8,128)(2,1)S(1)} %all_to_all.17.got_ref), custom_call_target="tpu_custom_call" | custom-call | tf_op jit(solution)/shard_map/pallas_call | solution.py:227
Async XLA Ops:
  20.7 10.3 %copy-start = (bf16[1024,256]{1,0:T(8,128)(2,1)S(1)}, bf16[1024,256]{1,0:T(8,128)(2,1)}, u32[]{:S(2)}) copy-start(bf16[1024,256]{1,0:T(8,128)(2,1)} %loadings_ref.1) | copy-start | bytes 1572868

commit v6 on v5

--- a/solution.py
+++ b/solution.py
@@ -15,8 +15,13 @@
 TILE, TILES = 4, 8
 
 
+def origin(core):
+    return 4 + 3 * core, 3 * core
+
+
 def member(z, core, y, x):
-    return ((y + core) % 8 * 4 + (x + core) % 4) * 16 + z * 2 + core
+    y_from, x_from = origin(core)
+    return ((y + y_from) % 8 * 4 + (x + x_from) % 4) * 16 + z * 2 + core
 
 
 FIRST = [
@@ -49,8 +54,9 @@
 
 
 def row_of(group, core):
-    y = ((group >> 6) - core) & 7
-    x = ((group >> 4) - core) & 3
+    y_from, x_from = origin(core)
+    y = ((group >> 6) - y_from) & 7
+    x = ((group >> 4) - x_from) & 3
     h, q = y >> 1, x >> 1
     y_set = (y ^ h ^ (h >> 1) ^ 1) & 1
     x_set = (x ^ q ^ 1) & 1

time: 57.5 us -> 55.1 us (0.958)
  blocking collectives: 52.4 us -> 49.9 us
    all_to_all x1, blocking collectives: 25.4 us -> 17.4 us  [shards(): got = lax.all_to_all(sent, 'gene', 0, 0, tiled=True)]
    all_to_all x2, blocking collectives: 27 us -> 32.5 us  [shards(): lax.all_to_all(sent, ('dp', 'gene'), 0, 0, tiled=True, axis_index_groups=...]
where the time goes in v6:
time: 55.1 us; the launch traced here: 54.9 us
  blocking collectives  49.9 us (91%)
  Pallas kernels  4.31 us (8%)
  between operations  0.65 us (1%)
    all_to_all x2, blocking collectives, shards(): lax.all_to_all(sent, ('dp', 'gene'), 0, 0, tiled=True, axis_index_groups=...  32.5 us
    all_to_all x1, blocking collectives, shards(): got = lax.all_to_all(sent, 'gene', 0, 0, tiled=True)  17.4 us
    pallas_call x1, Pallas kernels, local_sums(): pl.pallas_call(sums_kernel, in_specs=[HBM, HBM, HBM], out_specs=VMEM, out...  3.19 us

profile of v6, /device:TPU:1, one launch (start us, length us, event | category | flops | bytes accessed | tf_op | source)
XLA Modules:
  0.0 54.9 jit_solution(6317763418530879646)
XLA Ops:
  0.6 3.2 %shard_map.59 = bf16[4,1040,128]{2,1,0:T(8,128)(2,1)S(1)} custom-call(s32[1024]{0:T(1024)} %labels_hbm.1, s32[1024]{0:T(1024)} %lib_hbm.1, s32[1024,1024]{1,0:T(8,128)} %counts_hbm.1), custom_call_target="tpu_custom_call" | custom-call | tf_op jit(solution)/shard_map/pallas_call | solution.py:192
  3.8 18.9 %all_to_all.15.got_ref = bf16[4,1040,128]{2,1,0:T(8,128)(2,1)S(1)} all-to-all(bf16[4,1040,128]{2,1,0:T(8,128)(2,1)S(1)} %shard_map.59), channel_id=1, replica_groups={{336,320,272,256},{352,368,288,304},{400,384,464,448},{416,432,480,496}..., dimensions={0} | all-to-all | bytes 2129920 | tf_op jit(solution)/shard_map/all_to_all | solution.py:215
  22.7 0.0 copy-start
  22.7 0.2 shard_map.60
  22.9 13.6 %all_to_all.16.got_ref = bf16[8,144,128]{2,1,0:T(8,128)(2,1)S(1)} all-to-all(bf16[8,144,128]{2,1,0:T(8,128)(2,1)S(1)} %shard_map.60), channel_id=1, replica_groups={{336,352,400,416,16,32,208,224},{320,368,384,432,0,48,192,240},{272,288..., dimensions={0} | all-to-all | bytes 589824 | tf_op jit(solution)/shard_map/all_to_all | solution.py:223
  36.5 0.0 copy-done
  36.5 0.3 shard_map.61
  36.8 17.4 %all_to_all.17.got_ref = bf16[16,16,128]{2,1,0:T(8,128)(2,1)S(1)} all-to-all(bf16[16,16,128]{2,1,0:T(8,128)(2,1)S(1)} %shard_map.61), channel_id=1, replica_groups=mesh['dp'=32,'gene'=16] {'gene'}, dimensions={0} | all-to-all | bytes 131072 | tf_op jit(solution)/shard_map/all_to_all | solution.py:232
  54.2 0.7 %shard_map.62 = (bf16[1,16384]{1,0:T(2,128)(2,1)}, f32[1,256]{1,0:T(1,128)}) custom-call(bf16[16,16,128]{2,1,0:T(8,128)(2,1)S(1)} %all_to_all.17.got_ref), custom_call_target="tpu_custom_call" | custom-call | tf_op jit(solution)/shard_map/pallas_call | solution.py:233
Async XLA Ops:
  22.7 13.8 %copy-start = (bf16[1024,256]{1,0:T(8,128)(2,1)S(1)}, bf16[1024,256]{1,0:T(8,128)(2,1)}, u32[]{:S(2)}) copy-start(bf16[1024,256]{1,0:T(8,128)(2,1)} %loadings_ref.1) | copy-start | bytes 1572868

commit v7 on v6

--- a/solution.py
+++ b/solution.py
@@ -16,7 +16,7 @@
 
 
 def origin(core):
-    return 4 + 3 * core, 3 * core
+    return 4 + 3 * core, 2 - core
 
 
 def member(z, core, y, x):

time: 55.1 us -> 54.1 us (0.982)
  blocking collectives: 49.9 us -> 48.9 us
    all_to_all x2, blocking collectives: 32.5 us -> 29.3 us  [shards(): lax.all_to_all(sent, ('dp', 'gene'), 0, 0, tiled=True, axis_index_groups=...]
    all_to_all x1, blocking collectives: 17.4 us -> 19.6 us  [shards(): got = lax.all_to_all(sent, 'gene', 0, 0, tiled=True)]
where the time goes in v7:
time: 54.1 us; the launch traced here: 53.9 us
  blocking collectives  48.9 us (90%)
  Pallas kernels  4.31 us (8%)
  between operations  0.65 us (1%)
    all_to_all x2, blocking collectives, shards(): lax.all_to_all(sent, ('dp', 'gene'), 0, 0, tiled=True, axis_index_groups=...  29.3 us
    all_to_all x1, blocking collectives, shards(): got = lax.all_to_all(sent, 'gene', 0, 0, tiled=True)  19.6 us
    pallas_call x1, Pallas kernels, local_sums(): pl.pallas_call(sums_kernel, in_specs=[HBM, HBM, HBM], out_specs=VMEM, out...  3.19 us

profile of v7, /device:TPU:1, one launch (start us, length us, event | category | flops | bytes accessed | tf_op | source)
XLA Modules:
  0.0 53.9 jit_solution(432700955095943986)
XLA Ops:
  0.6 3.2 %shard_map.59 = bf16[4,1040,128]{2,1,0:T(8,128)(2,1)S(1)} custom-call(s32[1024]{0:T(1024)} %labels_hbm.1, s32[1024]{0:T(1024)} %lib_hbm.1, s32[1024,1024]{1,0:T(8,128)} %counts_hbm.1), custom_call_target="tpu_custom_call" | custom-call | tf_op jit(solution)/shard_map/pallas_call | solution.py:192
  3.8 16.8 %all_to_all.15.got_ref = bf16[4,1040,128]{2,1,0:T(8,128)(2,1)S(1)} all-to-all(bf16[4,1040,128]{2,1,0:T(8,128)(2,1)S(1)} %shard_map.59), channel_id=1, replica_groups={{368,352,304,288},{320,336,256,272},{432,416,496,480},{384,400,448,464}..., dimensions={0} | all-to-all | bytes 2129920 | tf_op jit(solution)/shard_map/all_to_all | solution.py:215
  20.7 0.0 copy-start
  20.7 0.2 shard_map.60
  20.8 12.4 %all_to_all.16.got_ref = bf16[8,144,128]{2,1,0:T(8,128)(2,1)S(1)} all-to-all(bf16[8,144,128]{2,1,0:T(8,128)(2,1)S(1)} %shard_map.60), channel_id=1, replica_groups={{368,320,432,384,48,0,240,192},{352,336,416,400,32,16,224,208},{304,256..., dimensions={0} | all-to-all | bytes 589824 | tf_op jit(solution)/shard_map/all_to_all | solution.py:223
  33.2 0.0 copy-done
  33.3 0.3 shard_map.61
  33.5 19.6 %all_to_all.17.got_ref = bf16[16,16,128]{2,1,0:T(8,128)(2,1)S(1)} all-to-all(bf16[16,16,128]{2,1,0:T(8,128)(2,1)S(1)} %shard_map.61), channel_id=1, replica_groups=mesh['dp'=32,'gene'=16] {'gene'}, dimensions={0} | all-to-all | bytes 131072 | tf_op jit(solution)/shard_map/all_to_all | solution.py:232
  53.2 0.7 %shard_map.62 = (bf16[1,16384]{1,0:T(2,128)(2,1)}, f32[1,256]{1,0:T(1,128)}) custom-call(bf16[16,16,128]{2,1,0:T(8,128)(2,1)S(1)} %all_to_all.17.got_ref), custom_call_target="tpu_custom_call" | custom-call | tf_op jit(solution)/shard_map/pallas_call | solution.py:233
Async XLA Ops:
  20.7 12.6 %copy-start = (bf16[1024,256]{1,0:T(8,128)(2,1)S(1)}, bf16[1024,256]{1,0:T(8,128)(2,1)}, u32[]{:S(2)}) copy-start(bf16[1024,256]{1,0:T(8,128)(2,1)} %loadings_ref.1) | copy-start | bytes 1572868

commit v8 on v7

--- a/solution.py
+++ b/solution.py
@@ -9,6 +9,7 @@
 F32 = jnp.float32
 BF16 = jnp.bfloat16
 LANES = 128
+HALF = 8
 OWN = 16
 Y_SETS = ((1, 2, 4, 7), (0, 3, 5, 6))
 X_SETS = ((1, 2), (0, 3))
@@ -138,26 +139,33 @@
         return sum(got_ref[m, row : row + OWN, :].astype(F32) for m in range(TILE))
 
     lane = lax.broadcasted_iota(jnp.int32, (OWN, LANES), 1)
+    half_lane = lax.broadcasted_iota(jnp.int32, (HALF, LANES), 1)
     library = added(tiles * TILES * OWN)
     for h in range(TILES):
         for t in range(tiles):
             out_ref[h, t * OWN : (t + 1) * OWN, :] = added((t * TILES + h) * OWN).astype(BF16)
         mine = jnp.sum(jnp.where(lane >> 3 == h, library, 0.0), axis=1, keepdims=True)
-        out_ref[h, tiles * OWN :, :] = in_lanes(split3(mine), lane).astype(BF16)
+        first = in_lanes(split3(mine[:HALF]), half_lane)
+        second = in_lanes(split3(mine[HALF:]), half_lane - 4)
+        out_ref[h, tiles * OWN :, :] = jnp.where(half_lane < 4, first, second).astype(BF16)
 
 
 def project_kernel(got_ref, loadings_ref, out_ref, rows_ref):
-    tiles = got_ref.shape[1] // OWN - 1
+    tiles = got_ref.shape[1] // OWN
     halves = loadings_ref.shape[1] // LANES
 
-    def added(t):
-        return sum(got_ref[h, t * OWN : (t + 1) * OWN, :].astype(F32) for h in range(TILES))
-
-    library = jnp.sum(added(tiles), axis=1, keepdims=True)
+    def added(row, rows):
+        return sum(got_ref[h, row : row + rows, :].astype(F32) for h in range(TILES))
+
+    lane = lax.broadcasted_iota(jnp.int32, (HALF, LANES), 1)
+    pieces = added(tiles * OWN, HALF)
+    first = jnp.sum(jnp.where(lane < 4, pieces, 0.0), axis=1, keepdims=True)
+    second = jnp.sum(jnp.where(lane < 4, 0.0, pieces), axis=1, keepdims=True)
+    library = jnp.concatenate([first, second], axis=0)
     rows_ref[...] = jnp.zeros_like(rows_ref)
     profile = []
     for t in range(tiles):
-        normalized = jnp.log(1.0 + 10000.0 * added(t) / library).astype(BF16)
+        normalized = jnp.log(1.0 + 10000.0 * added(t * OWN, OWN) / library).astype(BF16)
         rows_ref[pl.ds(t, OWN, stride=OWN), :] = normalized.astype(F32)
         profile.append(normalized)
     scores = jnp.dot(jnp.concatenate(profile, axis=1), loadings_ref[...], preferred_element_type=F32)
@@ -217,7 +225,7 @@
         middle_kernel,
         in_specs=[VMEM],
         out_specs=VMEM,
-        out_shape=jax.ShapeDtypeStruct((TILES, tiles * OWN + OWN, LANES), BF16),
+        out_shape=jax.ShapeDtypeStruct((TILES, tiles * OWN + HALF, LANES), BF16),
         compiler_params=pltpu.CompilerParams(vmem_limit_bytes=LIMIT),
     )(got)
     got = lax.all_to_all(sent, ("dp", "gene"), 0, 0, tiled=True, axis_index_groups=SECOND)

time: 54.1 us -> 53.9 us (level)
  no operation moved by 1% of the time
where the time goes in v8:
time: 53.9 us; the launch traced here: 53.7 us
  blocking collectives  48.6 us (90%)
  Pallas kernels  4.41 us (8%)
  between operations  0.65 us (1%)
    all_to_all x2, blocking collectives, shards(): lax.all_to_all(sent, ('dp', 'gene'), 0, 0, tiled=True, axis_index_groups=...  28.9 us
    all_to_all x1, blocking collectives, shards(): got = lax.all_to_all(sent, 'gene', 0, 0, tiled=True)  19.8 us
    pallas_call x1, Pallas kernels, local_sums(): pl.pallas_call(sums_kernel, in_specs=[HBM, HBM, HBM], out_specs=VMEM, out...  3.19 us

profile of v8, /device:TPU:1, one launch (start us, length us, event | category | flops | bytes accessed | tf_op | source)
XLA Modules:
  0.0 53.7 jit_solution(8209931219405482739)
XLA Ops:
  0.6 3.2 %shard_map.59 = bf16[4,1040,128]{2,1,0:T(8,128)(2,1)S(1)} custom-call(s32[1024]{0:T(1024)} %labels_hbm.1, s32[1024]{0:T(1024)} %lib_hbm.1, s32[1024,1024]{1,0:T(8,128)} %counts_hbm.1), custom_call_target="tpu_custom_call" | custom-call | tf_op jit(solution)/shard_map/pallas_call | solution.py:200
  3.8 16.8 %all_to_all.15.got_ref = bf16[4,1040,128]{2,1,0:T(8,128)(2,1)S(1)} all-to-all(bf16[4,1040,128]{2,1,0:T(8,128)(2,1)S(1)} %shard_map.59), channel_id=1, replica_groups={{368,352,304,288},{320,336,256,272},{432,416,496,480},{384,400,448,464}..., dimensions={0} | all-to-all | bytes 2129920 | tf_op jit(solution)/shard_map/all_to_all | solution.py:223
  20.7 0.0 copy-start
  20.7 0.2 shard_map.60
  20.8 12.0 %all_to_all.16.got_ref = bf16[8,136,128]{2,1,0:T(8,128)(2,1)S(1)} all-to-all(bf16[8,136,128]{2,1,0:T(8,128)(2,1)S(1)} %shard_map.60), channel_id=1, replica_groups={{368,320,432,384,48,0,240,192},{352,336,416,400,32,16,224,208},{304,256..., dimensions={0} | all-to-all | bytes 557056 | tf_op jit(solution)/shard_map/all_to_all | solution.py:231
  32.9 0.0 copy-done
  32.9 0.4 shard_map.61
  33.2 19.8 %all_to_all.17.got_ref = bf16[16,16,128]{2,1,0:T(8,128)(2,1)S(1)} all-to-all(bf16[16,16,128]{2,1,0:T(8,128)(2,1)S(1)} %shard_map.61), channel_id=1, replica_groups=mesh['dp'=32,'gene'=16] {'gene'}, dimensions={0} | all-to-all | bytes 131072 | tf_op jit(solution)/shard_map/all_to_all | solution.py:240
  53.0 0.7 %shard_map.62 = (bf16[1,16384]{1,0:T(2,128)(2,1)}, f32[1,256]{1,0:T(1,128)}) custom-call(bf16[16,16,128]{2,1,0:T(8,128)(2,1)S(1)} %all_to_all.17.got_ref), custom_call_target="tpu_custom_call" | custom-call | tf_op jit(solution)/shard_map/pallas_call | solution.py:241
Async XLA Ops:
  20.7 12.2 %copy-start = (bf16[1024,256]{1,0:T(8,128)(2,1)S(1)}, bf16[1024,256]{1,0:T(8,128)(2,1)}, u32[]{:S(2)}) copy-start(bf16[1024,256]{1,0:T(8,128)(2,1)} %loadings_ref.1) | copy-start | bytes 1572868

commit v9 on v7

--- a/solution.py
+++ b/solution.py
@@ -178,7 +178,7 @@
         total += block
         for t in range(tiles):
             at = (source * tiles + t) * LANES
-            profile_ref[:, at : at + LANES] = block[t : t + 1].astype(BF16)
+            profile_ref[:, at : at + LANES] = got_ref[source, t : t + 1, :]
     for k in range(halves):
         scores_ref[:, k * LANES : (k + 1) * LANES] = sum(
             total[tiles + p * halves + k : tiles + p * halves + k + 1] for p in range(3)

time: 54.1 us -> 54.1 us (level)
  no operation moved by 1% of the time
where the time goes in v9:
time: 54.1 us; the launch traced here: 53.9 us
  blocking collectives  48.9 us (90%)
  Pallas kernels  4.34 us (8%)
  between operations  0.65 us (1%)
    all_to_all x2, blocking collectives, shards(): lax.all_to_all(sent, ('dp', 'gene'), 0, 0, tiled=True, axis_index_groups=...  29.3 us
    all_to_all x1, blocking collectives, shards(): got = lax.all_to_all(sent, 'gene', 0, 0, tiled=True)  19.6 us
    pallas_call x1, Pallas kernels, local_sums(): pl.pallas_call(sums_kernel, in_specs=[HBM, HBM, HBM], out_specs=VMEM, out...  3.19 us

profile of v9, /device:TPU:1, one launch (start us, length us, event | category | flops | bytes accessed | tf_op | source)
XLA Modules:
  0.0 53.9 jit_solution(5582710316814779196)
XLA Ops:
  0.6 3.2 %shard_map.59 = bf16[4,1040,128]{2,1,0:T(8,128)(2,1)S(1)} custom-call(s32[1024]{0:T(1024)} %labels_hbm.1, s32[1024]{0:T(1024)} %lib_hbm.1, s32[1024,1024]{1,0:T(8,128)} %counts_hbm.1), custom_call_target="tpu_custom_call" | custom-call | tf_op jit(solution)/shard_map/pallas_call | solution.py:192
  3.8 16.8 %all_to_all.15.got_ref = bf16[4,1040,128]{2,1,0:T(8,128)(2,1)S(1)} all-to-all(bf16[4,1040,128]{2,1,0:T(8,128)(2,1)S(1)} %shard_map.59), channel_id=1, replica_groups={{368,352,304,288},{320,336,256,272},{432,416,496,480},{384,400,448,464}..., dimensions={0} | all-to-all | bytes 2129920 | tf_op jit(solution)/shard_map/all_to_all | solution.py:215
  20.7 0.0 copy-start
  20.7 0.2 shard_map.60
  20.8 12.4 %all_to_all.16.got_ref = bf16[8,144,128]{2,1,0:T(8,128)(2,1)S(1)} all-to-all(bf16[8,144,128]{2,1,0:T(8,128)(2,1)S(1)} %shard_map.60), channel_id=1, replica_groups={{368,320,432,384,48,0,240,192},{352,336,416,400,32,16,224,208},{304,256..., dimensions={0} | all-to-all | bytes 589824 | tf_op jit(solution)/shard_map/all_to_all | solution.py:223
  33.2 0.0 copy-done
  33.3 0.3 shard_map.61
  33.5 19.6 %all_to_all.17.got_ref = bf16[16,16,128]{2,1,0:T(8,128)(2,1)S(1)} all-to-all(bf16[16,16,128]{2,1,0:T(8,128)(2,1)S(1)} %shard_map.61), channel_id=1, replica_groups=mesh['dp'=32,'gene'=16] {'gene'}, dimensions={0} | all-to-all | bytes 131072 | tf_op jit(solution)/shard_map/all_to_all | solution.py:232
  53.2 0.7 %shard_map.62 = (bf16[1,16384]{1,0:T(2,128)(2,1)}, f32[1,256]{1,0:T(1,128)}) custom-call(bf16[16,16,128]{2,1,0:T(8,128)(2,1)S(1)} %all_to_all.17.got_ref), custom_call_target="tpu_custom_call" | custom-call | tf_op jit(solution)/shard_map/pallas_call | solution.py:233
Async XLA Ops:
  20.7 12.6 %copy-start = (bf16[1024,256]{1,0:T(8,128)(2,1)S(1)}, bf16[1024,256]{1,0:T(8,128)(2,1)}, u32[]{:S(2)}) copy-start(bf16[1024,256]{1,0:T(8,128)(2,1)} %loadings_ref.1) | copy-start | bytes 1572868
